TPU v7x, 128 devices: a whole 4x4x4 slice. The times are simulated.
128 devices in a mesh: grp: 8 (over z, core), own: 16 (over y, x).
Axes of the slice: x: 4, y: 4, z: 4, core: 2. Of those that a mesh axis runs over, the one named last changes fastest.
Arguments:
- vectors: bfloat16 [32768, 768], P(('grp', 'own')), may hold values from -64 to 64
- candidates: int32 [32768, 8], P(('grp', 'own')), may hold values from 0 to 511, all different within a row; in each aligned block of 256 rows (0 to 255, 256 to 511, ...) at most 8 rows name the same one
- centroids: bfloat16 [65536, 768], P('own'), may hold values from -8 to 8
Outputs:
- refined: bfloat16 [65536, 768], P('own')
Inputs may be any that keep to these rules, and one draw needn't show every extreme that they name: `candidates`: the 8 cells named by one vector are distinct. Among the vectors of one device no cell is named by more than 8 of them, and in every draw some cell is named by exactly 8.
All inputs are finite; a program needn't handle non-finite values.
Results may differ from a plain program's by a relative error of at most 0.006.
Values may be sent and summed in bfloat16 or wider, within the bound.
A program may use at most 128 MiB of HBM per device.

v0:
```python
import functools

import jax
import jax.numpy as jnp
from jax import lax
from jax.experimental import pallas as pl
from jax.experimental.pallas import tpu as pltpu
from jax.sharding import PartitionSpec as P

MESH = pl.DeviceIdType.MESH
F32 = jnp.float32
BF16 = jnp.bfloat16

CELL = 128
SLOTS = 8
VEC = 256
D = 768
SIDE = 4
PLANE = SIDE * SIDE
SRC = 2 * PLANE
MINE = 16
QUARTER = MINE // SIDE
ROWS = SRC * SLOTS
ROUTED = 2
PRIOR_MASS = 1.0
LOW = -1e30
HIGH = 1e30

HALF = VEC // 2
FOURTH = VEC // 4


BUDGET = 1.0
SPOTS = (
    (0, 0), (1, 0), (-1, 0), (0, 1), (0, -1), (1, 1), (2, 0), (0, 2),
    (1, -1), (-1, 1), (-1, -1), (2, 1), (1, 2), (2, -1), (-1, 2), (2, 2),
)
GROUPS = ((0, 5), (5, 6), (11, 2), (13, 3))
LATE = 13
FRESH = 2 * (PLANE - LATE)


def mirrored(place):
    dx, dy = (0 if v == 0 else 2 if v == 2 else -v for v in SPOTS[place])
    return SPOTS.index((dx, dy))


def behind(place, late):
    dx, dy = ((a - b + 5) % 4 - 1 for a, b in zip(SPOTS[place], SPOTS[late]))
    return SPOTS.index((dx, dy))


def ring(i):
    return lax.rem(i + 2 * SIDE, SIDE)


def kernel(
    vec, cand, cents, out,
    X, CD, CE, C, CT, R, RK, H, U, SQ, L, LB, LVS, PV, LV2, LT, MS, MR, S, SF, RN, RP,
    R3, SHR, SHZ, SQC,
    rows_send, rows_recv, shift_send, shift_recv, load_sem, cand_send, cand_recv, ag_send, ag_recv, sib_send, sib_recv, lse_sem,
    rs_send, rs_recv, mass_sem, og_send, og_recv, os_send, os_recv,
):
    grp = lax.axis_index("grp")
    own = lax.axis_index("own")
    z, k = lax.div(grp, 2), lax.rem(grp, 2)
    y, x = lax.div(own, SIDE), lax.rem(own, SIDE)
    sibling = (z * 2 + 1 - k, own)
    z_next = (ring(z + 1) * 2 + k, own)
    z_prev = (ring(z - 1) * 2 + k, own)
    z_far = (ring(z + 2) * 2 + k, own)
    me = k * PLANE + own
    both = (0, 1)
    last = (((1,), (1,)), ((), ()))

    def at(dx, dy):
        return ring(y + dy) * SIDE + ring(x + dx)

    def remote(src, dst, send, recv, device):
        return pltpu.make_async_remote_copy(
            src_ref=src, dst_ref=dst, send_sem=send, recv_sem=recv,
            device_id=device, device_id_type=MESH,
        )

    loads = [
        pltpu.make_async_copy(vec, X.at[me], load_sem.at[0]),
        pltpu.make_async_copy(cand, CD.at[me], load_sem.at[1]),
        pltpu.make_async_copy(cents.at[pl.ds(k * MINE, MINE)], C, load_sem.at[2]),
    ]
    for load in loads:
        load.start()
    x_next, x_prev = (grp, at(1, 0)), (grp, at(-1, 0))
    y_next, y_prev = (grp, at(0, 1)), (grp, at(0, -1))
    x_far, y_far = (grp, at(2, 0)), (grp, at(0, 2))
    near = (x_next, x_prev, x_far, y_next, y_prev, y_far, sibling, z_next, z_prev, z_far)
    barrier = pltpu.get_barrier_semaphore()
    for device in near:
        pl.semaphore_signal(barrier, inc=1, device_id=device, device_id_type=MESH)
    pl.semaphore_wait(barrier, len(near))

    def block(h, first, second):
        return at(first, second) if h == 0 else at(second, first)

    def axis_peer(h, stage, step):
        along_x = (h == 0) == (stage == 1)
        return (grp, at(step, 0) if along_x else at(0, step))

    def rows_of(h, part):
        if part == 2:
            return pl.ds(h * HALF, HALF)
        return pl.ds(h * HALF + part * FOURTH, FOURTH)

    def message(h, stage, d, kind):
        place = 0 if stage == 1 else 1 + d % 4
        number = 4 * place + kind
        step = 1 if kind in (0, 2) else -1
        back = 0 if kind < 2 else -step
        blk = block(h, back, 0) if stage == 1 else block(h, d, back)
        ref = X.at[k * PLANE + blk, rows_of(h, 2 if kind < 2 else kind - 2)]
        return remote(
            ref, ref, ag_send.at[h, number], ag_recv.at[h, number], axis_peer(h, stage, step)
        )

    def start(stage, d, kinds):
        for kind in kinds:
            for h in both:
                message(h, stage, d, kind).start()

    def to_sibling(h, place):
        ref = X.at[k * PLANE + at(*SPOTS[place]), rows_of(h, 2)]
        return remote(ref, ref, sib_send.at[h, place], sib_recv.at[h, place], sibling)

    def pass_on(h, first, second):
        to_sibling(h, SPOTS.index((first, second) if h == 0 else (second, first))).start()

    def arrive(stage, d, kinds, h):
        for kind in kinds:
            message(h, stage, d, kind).wait_recv()
            if kind < 2:
                side = -1 if kind == 0 else 1
                message(h, stage, d, 2 + kind).start()
                if stage == 1:
                    pass_on(h, side, 0)
                else:
                    pass_on(h, d, side)
        if kinds[-1] == 3:
            if stage == 1:
                pass_on(h, 2, 0)
            else:
                pass_on(h, d, 2)

    def take(places):
        for place in places:
            for h in both:
                to_sibling(h, place).wait_recv()

    def cand_message(number):
        if number < 3:
            ref = CD.at[pl.ds(k * PLANE + own, 1)]
            device = (x_next, x_prev, x_far)[number]
        else:
            ref = CD.at[pl.ds(k * PLANE + y * SIDE, SIDE)]
            device = (y_next, y_prev, y_far)[number - 3]
        return remote(ref, ref, cand_send.at[number], cand_recv.at[number], device)

    group_cand = CD.at[pl.ds(k * PLANE, PLANE)]
    cand_over = remote(group_cand, group_cand, cand_send.at[6], cand_recv.at[6], sibling)

    cand_near = remote(CD.at[me], CE, cand_send.at[7], cand_recv.at[7], sibling)

    def cand_start(numbers):
        for number in numbers:
            cand_message(number).start()

    def cand_arrive(numbers):
        for number in numbers:
            cand_message(number).wait_recv()

    column = (z_next, z_prev, z_far)
    column_step = (1, -1, 2)

    def rows_message(place, j):
        slots = pl.ds(place * 2 * SLOTS, 2 * SLOTS)
        cells = pl.ds(ring(z + column_step[j]) * QUARTER + (QUARTER - ROUTED), ROUTED)
        return remote(
            R.at[cells, slots], R3.at[j, :, slots], rows_send.at[j, place], rows_recv.at[j, place],
            column[j],
        )

    def shift_message(j):
        return remote(SHR.at[j], SHZ.at[j], shift_send.at[j], shift_recv.at[j], column[j])

    def turned(first, count):
        if not first:
            loads[2].wait()
        for c in range(first, first + count):
            block_t = C[c].T
            CT[c] = block_t
            value = block_t.astype(F32)
            SQ[c] = jnp.broadcast_to(jnp.sum(value * value, axis=0, keepdims=True), (8, CELL))

    def own_norms():
        for j in range(ROUTED):
            value = C[z * QUARTER + (QUARTER - ROUTED) + j].astype(F32)
            SQC[j] = jnp.broadcast_to(
                jnp.sum(value * value, axis=1, keepdims=True), (CELL, CELL)
            )

    def triangle():
        U[...] = jnp.where(
            lax.broadcasted_iota(jnp.int32, (VEC, VEC), 0)
            < lax.broadcasted_iota(jnp.int32, (VEC, VEC), 1),
            1.0,
            0.0,
        ).astype(BF16)

    def ranks(kk):
        labels = lax.broadcasted_iota(jnp.int32, (MINE, VEC), 0) + (own * 2 + k) * MINE
        for place, spot in enumerate(SPOTS):
            named = CD[kk * PLANE + at(*spot)]
            hit = named[0:1] == labels
            for i in range(1, 8):
                hit = hit | (named[i : i + 1] == labels)
            H[place * MINE : (place + 1) * MINE] = jnp.where(hit, 1.0, 0.0).astype(BF16)
        hits = H[...]
        rank = jnp.dot(hits, U[...], preferred_element_type=F32)
        slot = jnp.where(hits.astype(F32) > 0.5, rank, -1.0)
        RK[:, kk] = slot.reshape(PLANE, MINE, VEC)

    def own_ranks():
        labels = lax.broadcasted_iota(jnp.int32, (MINE, VEC), 0) + (own * 2 + k) * MINE
        for j, named in enumerate((CD[me], CE[...])):
            hit = named[0:1] == labels
            for i in range(1, 8):
                hit = hit | (named[i : i + 1] == labels)
            H[j * MINE : (j + 1) * MINE] = jnp.where(hit, 1.0, 0.0).astype(BF16)
        hits = H[0 : 2 * MINE]
        rank = jnp.dot(hits, U[...], preferred_element_type=F32)
        slot = jnp.where(hits.astype(F32) > 0.5, rank, -1.0)
        RK[0, k] = slot[0:MINE]
        RK[0, 1 - k] = slot[MINE:]

    def numbers(count):
        return lax.broadcasted_iota(jnp.int32, (count, SLOTS, VEC), 1).astype(F32)

    def slot_mask(place, kk):
        return RK[place, kk][:, None, :] == numbers(MINE)

    def place_rows(place):
        parts = []
        for kk in both:
            pick = jnp.where(slot_mask(place, kk), 1.0, 0.0).reshape(MINE * SLOTS, VEC)
            rows = jnp.dot(
                pick.astype(BF16), X[kk * PLANE + at(*SPOTS[place])], preferred_element_type=F32
            )
            parts.append(rows.reshape(MINE, SLOTS, D))
        base = place * 2 * SLOTS
        R[:, base : base + 2 * SLOTS, :] = jnp.concatenate(parts, axis=1).astype(BF16)
        for j in (2, 0, 1):
            rows_message(place, j).start()

    def logits(group, first_cell, cells):
        first, count = GROUPS[group]
        slots = slice(first * 2 * SLOTS, (first + count) * 2 * SLOTS)
        for c in range(first_cell, first_cell + cells):
            products = jnp.dot(R[c, slots], CT[c], preferred_element_type=F32)
            value = (2.0 * products - SQ[c][0:1]) * D**-0.5
            L[c, slots] = value
            top = jnp.max(value, axis=1, keepdims=True)
            total = jnp.sum(jnp.exp(value - top), axis=1, keepdims=True)
            LB[c, slots] = jnp.broadcast_to(top + jnp.log(total), (count * 2 * SLOTS, CELL))

    def partial(place):
        for kk in both:
            base = (place * 2 + kk) * SLOTS
            part = LB[:, base : base + SLOTS, :]
            wide = jnp.concatenate([part, part], axis=2)
            mask = slot_mask(place, kk)
            known = jnp.where(mask, wide, LOW)
            top = jnp.max(jnp.max(known, axis=0), axis=0, keepdims=True)
            terms = jnp.where(mask, jnp.exp(known - top[None]), 0.0)
            total = jnp.sum(jnp.sum(terms, axis=0), axis=0, keepdims=True)
            LVS[2 * place + kk] = top + jnp.log(jnp.maximum(total, 1e-30))
            if 0 < place < LATE:
                device = (z * 2 + kk, at(*SPOTS[place]))
                send_partial(2 * place + kk, 2 * place + k, device)
        if not place:
            PV[k] = LVS[k]
            send_partial(1 - k, k, sibling)

    def send_partial(number, there, device):
        remote(LVS.at[number], PV.at[there], lse_sem.at[0], lse_sem.at[1], device).start()

    def announce(src, dst, send, recv):
        for place in range(PLANE - 1, 0, -1):
            for kk in both:
                device = (z * 2 + kk, at(*SPOTS[place]))
                remote(src, dst.at[2 * mirrored(place) + k], send, recv, device).start()
        remote(src, dst.at[k], send, recv, sibling).start()

    loads[1].wait()
    cand_start((0, 1, 2))
    cand_near.start()
    loads[0].wait()
    start(1, 0, (0, 1))
    for h in both:
        pass_on(h, 0, 0)
    triangle()
    cand_arrive((0, 1, 2))
    cand_start((3, 4, 5))
    start(2, 0, (0, 1))
    cand_near.wait_recv()
    own_ranks()
    take((0,))
    place_rows(0)

    steps = []
    for h in both:
        steps.append(("", functools.partial(arrive, 1, 0, (0, 1), h)))
    steps.append(("", lambda: start(2, 1, (0, 1))))
    steps.append(("", lambda: cand_arrive((3, 4, 5))))
    steps.append(("cand", cand_over.start))
    for h in both:
        steps.append(("ring1" if h else "", functools.partial(arrive, 2, 0, (0, 1), h)))
    steps.append(("over", lambda: start(2, -1, (0, 1))))
    for h in both:
        steps.append(("", functools.partial(arrive, 1, 0, (2, 3), h)))
    steps.append(("", lambda: start(2, 2, (0, 1))))
    for h in both:
        for kinds in ((0,), (1,)):
            name = "ring2" if h and kinds[0] else ""
            steps.append((name, functools.partial(arrive, 2, 1, kinds, h)))
    for h in both:
        steps.append(("far1" if h else "", functools.partial(arrive, 2, 0, (2, 3), h)))
    for h in both:
        for kinds in ((0,), (1,)):
            name = "ring3" if h and kinds[0] else ""
            steps.append((name, functools.partial(arrive, 2, -1, kinds, h)))
    for h in both:
        for kinds in ((0,), (1,)):
            steps.append(("", functools.partial(arrive, 2, 2, kinds, h)))
    for d in (1, -1):
        for h in both:
            name = "" if not h else "far2" if d > 0 else "far3"
            steps.append((name, functools.partial(arrive, 2, d, (2, 3), h)))
    for h in both:
        steps.append(("end" if h else "", functools.partial(arrive, 2, 2, (2, 3), h)))

    placing, scoring = [], []
    for c in range(0, MINE, 2):
        scoring.append(("", functools.partial(turned, c, 2), 0.5))
    scoring.append(("", own_norms, 0.3))

    def ranks_of_other():
        cand_over.wait_recv()
        ranks(1 - k)

    placing.append(("cand", lambda: ranks(k), 1.0))
    placing.append(("over", ranks_of_other, 1.0))

    def placed(places, ready):
        placing.append((ready, functools.partial(take, places), 0.0))
        for place in places:
            placing.append((ready, functools.partial(place_rows, place), 0.4))

    def scored(group, ready):
        for c in range(0, MINE, 4):
            scoring.append((ready, functools.partial(logits, group, c, 4), 0.3))
        first, count = GROUPS[group]
        for place in range(first, first + count):
            scoring.append((ready, functools.partial(partial, place), 0.2))

    done = {"", ("placed", 0)}
    placed((1, 2, 3, 4), "ring1")
    placed((5,), "ring2")
    placed((6, 7), "far1")
    placed((8, 9, 10), "ring3")
    placed((11, 12), "far2")
    placed((13, 14), "far3")
    placed((15,), "end")
    scored(0, ("placed", 4))
    scored(1, ("placed", 10))
    scored(2, ("placed", 12))


    def advance(works, spent):
        while works and works[0][0] in done and spent < BUDGET:
            _, work, cost = works.pop(0)
            work()
            spent += cost
            if work.__class__ is functools.partial and work.func is place_rows:
                done.add(("placed", work.args[0]))
        return spent

    for name, step in steps:
        if step is not None:
            step()
        done.add(name)
        advance(scoring, advance(placing, 0.0))
    for works in (placing, scoring):
        for _, work, _ in works:
            work()
    logits(len(GROUPS) - 1, 0, MINE)
    for place in range(LATE, PLANE):
        partial(place)

    others = PV.at[pl.ds(0, 2 * LATE - 1)]
    pltpu.make_async_copy(others, others, lse_sem.at[1]).wait()
    parts = PV[...]
    top = jnp.max(parts, axis=0, keepdims=True)
    LVS[SRC : SRC + 1] = top + jnp.log(jnp.sum(jnp.exp(parts - top), axis=0, keepdims=True))
    LT[k] = LVS[SRC - FRESH :]
    announce(LVS.at[pl.ds(SRC - FRESH, FRESH + 1)], LT, lse_sem.at[2], lse_sem.at[3])
    others = LT.at[pl.ds(0, SRC - 1)]
    pltpu.make_async_copy(others, others, lse_sem.at[3]).wait()
    for place in range(PLANE):
        for kk in both:
            terms = [LT[2 * place + kk, FRESH]]
            for late in range(LATE, PLANE):
                for core in both:
                    terms.append(LT[2 * behind(place, late) + core, 2 * (late - LATE) + kk])
            top = functools.reduce(jnp.maximum, terms)
            LV2[2 * place + kk] = top + jnp.log(sum(jnp.exp(v - top) for v in terms))

    def cell_shift(c):
        rank = RK[:, :, pl.ds(c, 1), :].reshape(SRC, 1, VEC)
        found = jnp.where(rank == numbers(SRC), LV2[...], HIGH)
        return jnp.min(found, axis=2, keepdims=True).reshape(ROWS, 1)

    def cell_sum(c):
        weights = jnp.exp(L[c] - cell_shift(c)).astype(BF16)
        MS[c] = jnp.sum(weights.astype(F32), axis=0, keepdims=True)
        return lax.dot_general(
            weights, R[c], (((0,), (0,)), ((), ())), preferred_element_type=F32
        )

    def cell_of(step, i):
        return ring(z + step) * QUARTER + i

    landing = (RN, RP)
    toward = (z_next, z_prev)

    def reduce_message(way, number):
        return remote(
            S.at[way, number], landing[way].at[number],
            rs_send.at[way, number], rs_recv.at[way, number], toward[way],
        )

    def out_cell(step, i):
        return out.at[k * MINE + cell_of(step, i)]

    def out_message(kind, i):
        ref = out_cell((0, 0, -1, 1)[kind], i)
        return remote(ref, ref, og_send.at[kind, i], og_recv.at[kind, i], toward[kind % 2])

    def out_sibling(step, i):
        ref = out_cell(step, i)
        return remote(ref, ref, os_send.at[step % 4, i], os_recv.at[step % 4, i], sibling)

    diagonal = lax.broadcasted_iota(jnp.int32, (CELL, CELL), 0) == lax.broadcasted_iota(
        jnp.int32, (CELL, CELL), 1
    )

    def finish(i, total, mass_row, mass):
        c = z * QUARTER + i
        mass = mass + jnp.sum(
            jnp.where(diagonal, jnp.broadcast_to(mass_row, (CELL, CELL)), 0.0),
            axis=1,
            keepdims=True,
        )
        out[k * MINE + c] = (
            (total + PRIOR_MASS * C[c].astype(F32)) / (mass + PRIOR_MASS)
        ).astype(BF16)
        out_message(0, i).start()
        out_message(1, i).start()
        out_sibling(0, i).start()

    eye = lax.broadcasted_iota(jnp.int32, (ROWS, ROWS), 0) == lax.broadcasted_iota(
        jnp.int32, (ROWS, ROWS), 1
    )
    for j in (2, 0, 1):
        for i in range(ROUTED):
            shift = cell_shift(cell_of(column_step[j], QUARTER - ROUTED + i))
            wide = jnp.where(eye, jnp.broadcast_to(shift, (ROWS, ROWS)), 0.0)
            SHR[j, i] = jnp.sum(wide, axis=0, keepdims=True)
        shift_message(j).start()

    for way in both:
        S[way, 0] = cell_sum(cell_of(2, way)).astype(BF16)
        reduce_message(way, 0).start()
    for way in both:
        S[way, 1] = cell_sum(cell_of(1 - 2 * way, 1 - way)).astype(BF16)
        reduce_message(way, 1).start()

    for way in both:
        SF[way] = cell_sum(cell_of(1 - 2 * way, way))

    def own_sum(i, carry):
        SF[2 + i] = cell_sum(z * QUARTER + i)
        return carry

    lax.fori_loop(0, QUARTER, own_sum, 0)
    MR[z] = MS[...]
    for j, device in enumerate((z_next, z_prev, z_far)):
        remote(MS, MR.at[z], mass_sem.at[j], mass_sem.at[3], device).start()
    for j in range(3):
        shift_message(j).wait_recv()
        for place in range(PLANE):
            rows_message(place, j).wait_recv()
    def finish_rows(i):
        c = z * QUARTER + (QUARTER - ROUTED) + i
        mass = 0.0
        total = SF[2 + QUARTER - ROUTED + i]
        for j in range(3):
            rows = R3[j, i]
            products = lax.dot_general(C[c], rows, last, preferred_element_type=F32)
            value = (2.0 * products - SQC[i][:, 0:1]) * D**-0.5
            weights = jnp.exp(value - SHZ[j, i]).astype(BF16)
            mass = mass + jnp.sum(weights.astype(F32), axis=1, keepdims=True)
            total = total + jnp.dot(weights, rows, preferred_element_type=F32)
        finish(QUARTER - ROUTED + i, total, MS[c], mass)

    finish_rows(0)
    for way in both:
        reduce_message(way, 0).wait_recv()
        S[way, 2] = (SF[way] + landing[way][0].astype(F32)).astype(BF16)
        reduce_message(way, 2).start()
    finish_rows(1)
    others = MR.at[pl.ds(0, SIDE - 1)]
    pltpu.make_async_copy(others, others, mass_sem.at[3]).wait()

    def out_arrive(i):
        for kind in both:
            out_message(kind, i).wait_recv()
            if i % 2 == kind:
                out_message(2 + kind, i).start()
            out_sibling(-1 if kind == 0 else 1, i).start()

    for h in both:
        for stage, d in ((1, 0), (2, 0), (2, 1), (2, -1), (2, 2)):
            for kind in range(4):
                message(h, stage, d, kind).wait_send()
        for place in range(PLANE):
            to_sibling(h, place).wait_send()
    for number in range(6):
        cand_message(number).wait_send()
    cand_over.wait_send()
    cand_near.wait_send()
    for j in range(3):
        shift_message(j).wait_send()
        for place in range(PLANE):
            rows_message(place, j).wait_send()
    sent = PV.at[pl.ds(0, 2 * LATE - 1)]
    pltpu.make_async_copy(sent, sent, lse_sem.at[0]).wait()
    sent = LT.at[pl.ds(0, SRC - 1)]
    pltpu.make_async_copy(sent, sent, lse_sem.at[2]).wait()
    out_arrive(2)
    for i in both:
        reduce_message(0, 2 - i).wait_recv()
        reduce_message(1, 1 + i).wait_recv()
        c = z * QUARTER + i
        total = SF[2 + i] + RN[2 - i].astype(F32) + RP[1 + i].astype(F32)
        finish(i, total, MR[0, c] + MR[1, c] + MR[2, c] + MR[3, c], 0.0)

    out_arrive(3)
    for way in both:
        for number in range(3):
            reduce_message(way, number).wait_send()
    for j, device in enumerate((z_next, z_prev, z_far)):
        remote(MS, MR.at[z], mass_sem.at[j], mass_sem.at[3], device).wait_send()
    for i in both:
        out_arrive(i)
    for i in (2, 3):
        out_message(2 + i % 2, i).wait_recv()
        out_sibling(2, i).start()
    for i in range(QUARTER):
        out_message(0, i).wait_send()
        out_message(1, i).wait_send()
        for step in (0, -1, 1):
            out_sibling(step, i).wait_send()
            out_sibling(step, i).wait_recv()
    for i in both:
        out_message(2 + i % 2, i).wait_recv()
        out_sibling(2, i).start()
    for i in (2, 3, 0, 1):
        out_message(2 + i % 2, i).wait_send()
        out_sibling(2, i).wait_send()
        out_sibling(2, i).wait_recv()


def body(vectors, candidates, centroids):
    cells = centroids.shape[0] // CELL
    dma = pltpu.SemaphoreType.DMA
    any_space = pl.BlockSpec(memory_space=pl.ANY)
    refined = pl.pallas_call(
        kernel,
        out_shape=pltpu.VMEM((cells, CELL, D), BF16),
        in_specs=[any_space] * 3,
        out_specs=pl.BlockSpec(memory_space=pltpu.VMEM),
        scratch_shapes=[
            pltpu.VMEM((SRC, VEC, D), BF16),
            pltpu.VMEM((SRC, 8, VEC), jnp.int32),
            pltpu.VMEM((8, VEC), jnp.int32),
            pltpu.VMEM((MINE, CELL, D), BF16),
            pltpu.VMEM((MINE, D, CELL), BF16),
            pltpu.VMEM((MINE, ROWS, D), BF16),
            pltpu.VMEM((PLANE, 2, MINE, VEC), F32),
            pltpu.VMEM((PLANE * MINE, VEC), BF16),
            pltpu.VMEM((VEC, VEC), BF16),
            pltpu.VMEM((MINE, 8, CELL), F32),
            pltpu.VMEM((MINE, ROWS, CELL), F32),
            pltpu.VMEM((MINE, ROWS, CELL), F32),
            pltpu.VMEM((SRC + 1, 1, VEC), F32),
            pltpu.VMEM((2 * LATE, 1, VEC), F32),
            pltpu.VMEM((SRC, 1, VEC), F32),
            pltpu.VMEM((SRC, FRESH + 1, 1, VEC), F32),
            pltpu.VMEM((MINE, 1, CELL), F32),
            pltpu.VMEM((SIDE, MINE, 1, CELL), F32),
            pltpu.VMEM((2, 3, CELL, D), BF16),
            pltpu.VMEM((2 + QUARTER, CELL, D), F32),
            pltpu.VMEM((3, CELL, D), BF16),
            pltpu.VMEM((3, CELL, D), BF16),
            pltpu.VMEM((3, ROUTED, ROWS, D), BF16),
            pltpu.VMEM((3, ROUTED, 1, ROWS), F32),
            pltpu.VMEM((3, ROUTED, 1, ROWS), F32),
            pltpu.VMEM((ROUTED, CELL, CELL), F32),
            dma((3, 16)),
            dma((3, 16)),
            dma((3,)),
            dma((3,)),
            dma((3,)),
            dma((8,)),
            dma((8,)),
            dma((2, 20)),
            dma((2, 20)),
            dma((2, 16)),
            dma((2, 16)),
            dma((4,)),
            dma((2, 3)),
            dma((2, 3)),
            dma((4,)),
            dma((4, 4)),
            dma((4, 4)),
            dma((4, 4)),
            dma((4, 4)),
        ],
        compiler_params=pltpu.CompilerParams(
            collective_id=0, has_side_effects=True, vmem_limit_bytes=48 * 1024 * 1024
        ),
        name="refine",
    )(vectors, candidates.T, centroids.reshape(cells, CELL, D))
    return refined.reshape(cells * CELL, D)


def solution(mesh):
    placed = (P(("grp", "own"), None), P(("grp", "own"), None), P("own", None))
    return jax.shard_map(
        body, mesh=mesh, in_specs=placed, out_specs=P("own", None), check_vma=False
    )
```

profile of v0, /device:TPU:1, one launch (start us, length us, event | category | flops | bytes accessed | tf_op | source)
XLA Modules:
  0.0 104.4 jit_solution(2303142890733234510)
XLA Ops:
  0.0 101.7 %refine.1 = bf16[32,128,768]{2,1,0:T(8,128)(2,1)S(1)} custom-call(bf16[256,768]{1,0:T(8,128)(2,1)} %vec.1, s32[8,256]{1,0:T(8,128)} %bitcast.5, bf16[32,128,768]{2,1,0:T(8,128)(2,1)} %bitcast.4), custom_call_target="tpu_custom_call" | custom-call | tf_op jit(solution)/shard_map/refine/pallas_call | solution.py:595
  101.7 2.7 %copy.5 = bf16[4096,768]{1,0:T(8,128)(2,1)} copy(bf16[4096,768]{1,0:T(8,128)(2,1)S(1)} %bitcast.3) | data formatting | bytes 12582912
where the time goes:
time: 105 us; the launch traced here: 104 us
  Pallas kernels  102 us (97%)
  local copies, waits for them, and re-layouts  2.71 us (3%)
    pallas_call x1, Pallas kernels, body(): pl.pallas_call(kernel, out_shape=pltpu.VMEM((cells, CELL, D), BF16), in_s...  102 us
    unnamed x1, local copies, waits for them, and re-layouts  2.71 us

commit v1 on v0

--- a/solution.py
+++ b/solution.py
@@ -30,7 +30,7 @@
 FOURTH = VEC // 4
 
 
-BUDGET = 1.0
+BUDGET = 1.6
 SPOTS = (
     (0, 0), (1, 0), (-1, 0), (0, 1), (0, -1), (1, 1), (2, 0), (0, 2),
     (1, -1), (-1, 1), (-1, -1), (2, 1), (1, 2), (2, -1), (-1, 2), (2, 2),
@@ -112,11 +112,12 @@
 
     def message(h, stage, d, kind):
         place = 0 if stage == 1 else 1 + d % 4
-        number = 4 * place + kind
-        step = 1 if kind in (0, 2) else -1
-        back = 0 if kind < 2 else -step
+        number = 4 * place + kind if kind < 4 else 16 + kind
+        step = 1 if kind % 2 == 0 else -1
+        back = -step if kind in (2, 3) else 0
+        part = (2, 2, 0, 1)[kind] if d != 2 else (0, 1, 0, 1, 1, 0)[kind]
         blk = block(h, back, 0) if stage == 1 else block(h, d, back)
-        ref = X.at[k * PLANE + blk, rows_of(h, 2 if kind < 2 else kind - 2)]
+        ref = X.at[k * PLANE + blk, rows_of(h, part)]
         return remote(
             ref, ref, ag_send.at[h, number], ag_recv.at[h, number], axis_peer(h, stage, step)
         )
@@ -141,8 +142,10 @@
                 message(h, stage, d, 2 + kind).start()
                 if stage == 1:
                     pass_on(h, side, 0)
-                else:
+                elif d != 2:
                     pass_on(h, d, side)
+            elif kind > 3:
+                pass_on(h, d, -1 if kind == 4 else 1)
         if kinds[-1] == 3:
             if stage == 1:
                 pass_on(h, 2, 0)
@@ -320,12 +323,13 @@
     steps.append(("", lambda: start(2, 1, (0, 1))))
     steps.append(("", lambda: cand_arrive((3, 4, 5))))
     steps.append(("cand", cand_over.start))
-    for h in both:
-        steps.append(("ring1" if h else "", functools.partial(arrive, 2, 0, (0, 1), h)))
-    steps.append(("over", lambda: start(2, -1, (0, 1))))
+    steps.append(("over", None))
+    for h in both:
+        steps.append(("", functools.partial(arrive, 2, 0, (0, 1), h)))
+    steps.append(("ring1", lambda: start(2, -1, (0, 1))))
     for h in both:
         steps.append(("", functools.partial(arrive, 1, 0, (2, 3), h)))
-    steps.append(("", lambda: start(2, 2, (0, 1))))
+    steps.append(("", lambda: start(2, 2, (0, 1, 4, 5))))
     for h in both:
         for kinds in ((0,), (1,)):
             name = "ring2" if h and kinds[0] else ""
@@ -339,6 +343,8 @@
     for h in both:
         for kinds in ((0,), (1,)):
             steps.append(("", functools.partial(arrive, 2, 2, kinds, h)))
+    for h in both:
+        steps.append(("", functools.partial(arrive, 2, 2, (4, 5), h)))
     for d in (1, -1):
         for h in both:
             name = "" if not h else "far2" if d > 0 else "far3"
@@ -348,8 +354,8 @@
 
     placing, scoring = [], []
     for c in range(0, MINE, 2):
-        scoring.append(("", functools.partial(turned, c, 2), 0.5))
-    scoring.append(("", own_norms, 0.3))
+        scoring.append(("ring1", functools.partial(turned, c, 2), 0.5))
+    scoring.append(("ring1", own_norms, 0.3))
 
     def ranks_of_other():
         cand_over.wait_recv()
@@ -396,7 +402,7 @@
         if step is not None:
             step()
         done.add(name)
-        advance(scoring, advance(placing, 0.0))
+        advance(scoring, advance(placing, -1.0 if name == "ring1" else 0.0))
     for works in (placing, scoring):
         for _, work, _ in works:
             work()
@@ -538,7 +544,7 @@
 
     for h in both:
         for stage, d in ((1, 0), (2, 0), (2, 1), (2, -1), (2, 2)):
-            for kind in range(4):
+            for kind in range(6 if d == 2 else 4):
                 message(h, stage, d, kind).wait_send()
         for place in range(PLANE):
             to_sibling(h, place).wait_send()
@@ -631,8 +637,8 @@
             dma((3,)),
             dma((8,)),
             dma((8,)),
-            dma((2, 20)),
-            dma((2, 20)),
+            dma((2, 22)),
+            dma((2, 22)),
             dma((2, 16)),
             dma((2, 16)),
             dma((4,)),

time: 105 us -> 103 us (0.981)
  Pallas kernels: 102 us -> 100 us
    pallas_call x1, Pallas kernels: 102 us -> 100 us  [body(): pl.pallas_call(kernel, out_shape=pltpu.VMEM((cells, CELL, D), BF16), in_s...]
where the time goes in v1:
time: 103 us
  Pallas kernels  100 us (97%)
  local copies, waits for them, and re-layouts  2.71 us (3%)
    pallas_call x1, Pallas kernels, body(): pl.pallas_call(kernel, out_shape=pltpu.VMEM((cells, CELL, D), BF16), in_s...  100 us
    unnamed x1, local copies, waits for them, and re-layouts  2.71 us

profile of v1, /device:TPU:1, one launch (start us, length us, event | category | flops | bytes accessed | tf_op | source)
XLA Modules:
  0.0 103.2 jit_solution(15483019220987100830)
XLA Ops:
  0.0 100.5 %refine.1 = bf16[32,128,768]{2,1,0:T(8,128)(2,1)S(1)} custom-call(bf16[256,768]{1,0:T(8,128)(2,1)} %vec.1, s32[8,256]{1,0:T(8,128)} %bitcast.5, bf16[32,128,768]{2,1,0:T(8,128)(2,1)} %bitcast.4), custom_call_target="tpu_custom_call" | custom-call | tf_op jit(solution)/shard_map/refine/pallas_call | solution.py:601
  100.5 2.7 %copy.5 = bf16[4096,768]{1,0:T(8,128)(2,1)} copy(bf16[4096,768]{1,0:T(8,128)(2,1)S(1)} %bitcast.3) | data formatting | bytes 12582912

commit v2 on v1

--- a/solution.py
+++ b/solution.py
@@ -526,11 +526,11 @@
             total = total + jnp.dot(weights, rows, preferred_element_type=F32)
         finish(QUARTER - ROUTED + i, total, MS[c], mass)
 
-    finish_rows(0)
     for way in both:
         reduce_message(way, 0).wait_recv()
         S[way, 2] = (SF[way] + landing[way][0].astype(F32)).astype(BF16)
         reduce_message(way, 2).start()
+    finish_rows(0)
     finish_rows(1)
     others = MR.at[pl.ds(0, SIDE - 1)]
     pltpu.make_async_copy(others, others, mass_sem.at[3]).wait()

time: 103 us -> 103 us (level)
  no operation moved by 1% of the time
where the time goes in v2:
time: 103 us
  Pallas kernels  100 us (97%)
  local copies, waits for them, and re-layouts  2.71 us (3%)
    pallas_call x1, Pallas kernels, body(): pl.pallas_call(kernel, out_shape=pltpu.VMEM((cells, CELL, D), BF16), in_s...  100 us
    unnamed x1, local copies, waits for them, and re-layouts  2.71 us

profile of v2, /device:TPU:1, one launch (start us, length us, event | category | flops | bytes accessed | tf_op | source)
XLA Modules:
  0.0 103.2 jit_solution(7378075526690521263)
XLA Ops:
  0.0 100.5 %refine.1 = bf16[32,128,768]{2,1,0:T(8,128)(2,1)S(1)} custom-call(bf16[256,768]{1,0:T(8,128)(2,1)} %vec.1, s32[8,256]{1,0:T(8,128)} %bitcast.5, bf16[32,128,768]{2,1,0:T(8,128)(2,1)} %bitcast.4), custom_call_target="tpu_custom_call" | custom-call | tf_op jit(solution)/shard_map/refine/pallas_call | solution.py:601
  100.5 2.7 %copy.5 = bf16[4096,768]{1,0:T(8,128)(2,1)} copy(bf16[4096,768]{1,0:T(8,128)(2,1)S(1)} %bitcast.3) | data formatting | bytes 12582912

commit v3 on v1

--- a/solution.py
+++ b/solution.py
@@ -481,6 +481,10 @@
         out_message(1, i).start()
         out_sibling(0, i).start()
 
+    for way in both:
+        S[way, 0] = cell_sum(cell_of(2, way)).astype(BF16)
+        reduce_message(way, 0).start()
+
     eye = lax.broadcasted_iota(jnp.int32, (ROWS, ROWS), 0) == lax.broadcasted_iota(
         jnp.int32, (ROWS, ROWS), 1
     )
@@ -491,9 +495,6 @@
             SHR[j, i] = jnp.sum(wide, axis=0, keepdims=True)
         shift_message(j).start()
 
-    for way in both:
-        S[way, 0] = cell_sum(cell_of(2, way)).astype(BF16)
-        reduce_message(way, 0).start()
     for way in both:
         S[way, 1] = cell_sum(cell_of(1 - 2 * way, 1 - way)).astype(BF16)
         reduce_message(way, 1).start()

time: 103 us -> 103 us (level)
  no operation moved by 1% of the time
where the time goes in v3:
time: 103 us
  Pallas kernels  100 us (97%)
  local copies, waits for them, and re-layouts  2.71 us (3%)
    pallas_call x1, Pallas kernels, body(): pl.pallas_call(kernel, out_shape=pltpu.VMEM((cells, CELL, D), BF16), in_s...  100 us
    unnamed x1, local copies, waits for them, and re-layouts  2.71 us

profile of v3, /device:TPU:1, one launch (start us, length us, event | category | flops | bytes accessed | tf_op | source)
XLA Modules:
  0.0 102.8 jit_solution(4313673711816417584)
XLA Ops:
  0.0 100.1 %refine.1 = bf16[32,128,768]{2,1,0:T(8,128)(2,1)S(1)} custom-call(bf16[256,768]{1,0:T(8,128)(2,1)} %vec.1, s32[8,256]{1,0:T(8,128)} %bitcast.5, bf16[32,128,768]{2,1,0:T(8,128)(2,1)} %bitcast.4), custom_call_target="tpu_custom_call" | custom-call | tf_op jit(solution)/shard_map/refine/pallas_call | solution.py:602
  100.1 2.7 %copy.5 = bf16[4096,768]{1,0:T(8,128)(2,1)} copy(bf16[4096,768]{1,0:T(8,128)(2,1)S(1)} %bitcast.3) | data formatting | bytes 12582912
